TPU v7x, 32 devices: a whole 2x2x4 slice. The times are simulated.
32 devices in a mesh: video: 4 (over y, x), seq: 8 (over z, core).
Axes of the slice: x: 2, y: 2, z: 4, core: 2. Of those that a mesh axis runs over, the one named last changes fastest.
Arguments:
- queries: bfloat16 [4096, 2048], P(('video', 'seq')), parts along dimension 0, may hold values from -80 to 80
- keys: bfloat16 [4096, 2048], P(('video', 'seq')), parts along dimension 0, may hold values from -5 to 5
- values: bfloat16 [4096, 2048], P(('video', 'seq')), parts along dimension 0, may hold values from -6 to 6
- history: bfloat16 [16, 2048], P(None, ('video', 'seq')), parts along dimension 1, may hold values from -6 to 6
- levels: int32 [32], P('video'), parts along dimension 0, may hold values from 2 to 16, as said below
- patch_two: bfloat16 [32, 3072], replicated, may hold values from -1 to 1
- patch_four: bfloat16 [64, 3072], replicated, may hold values from -0.75 to 0.75
- patch_sixteen: bfloat16 [256, 3072], replicated, may hold values from -0.375 to 0.375
- mod_scale: float32 [3072], replicated, may hold values from -0.5 to 0.5
- mod_shift: float32 [3072], replicated, may hold values from -4 to 4
- kv_weight: bfloat16 [3072, 4096], P(None, 'seq'), may hold values from -0.109375 to 0.109375
- key_gain: float32 [128], replicated, may hold values from 0.5 to 2
Outputs:
- attended: bfloat16 [4096, 2048], P(('video', 'seq')), parts along dimension 0
There are 4 independent parts, one for each index of `video`. A program takes and returns all parts, laid end to end along the dimension named above; an argument that names none is the same for every part. Nothing has to cross between parts.
Inputs may be any that keep to these rules, and one draw needn't show every extreme that they name: `levels`: each aligned group of four devices holds the factors 2, 4, 4 and 16 in some order, so that one device's block gives at most 32 history tokens.
All inputs are finite; a program needn't handle non-finite values.
Results may differ from a plain program's by a relative error of at most 0.0034.
Values may be sent and summed in bfloat16 or wider, within the bound.
A program may use at most 128 MiB of HBM per device.

v0:
```python
import jax
import jax.numpy as jnp
from jax import lax
from jax.sharding import PartitionSpec as P

EPS = 1e-06


def divisor_near(total, target):
    parts = max(1, -(-total // target))
    while total % parts != 0:
        parts += 1
    return parts


def key_normed(pairs, gain):
    first = pairs[..., 0, :].astype(jnp.float32)
    scaled = first * lax.rsqrt(jnp.mean(first * first, axis=-1, keepdims=True) + EPS) * gain
    return jnp.concatenate([scaled.astype(jnp.bfloat16), pairs[..., 1, :]], axis=-1)


def level_tokens(everything, weight, level):
    channels, width = everything.shape
    grouped = (
        everything.reshape(channels, width // level, level)
        .transpose(1, 0, 2)
        .reshape(width // level, channels * level)
    )
    return jnp.dot(grouped, weight, preferred_element_type=jnp.float32).astype(jnp.bfloat16)


def history_rows(levels, positions):
    groups = levels.shape[0]
    counts = positions // levels
    ends = jnp.cumsum(counts)
    starts = ends - counts
    block_ids = jnp.arange(groups, dtype=jnp.int32)
    rows_total = 17 * positions * groups // 64
    place = jnp.arange(rows_total, dtype=jnp.int32)
    owner = jnp.sum((ends[None, :] <= place[:, None]).astype(jnp.int32), axis=1)
    match = owner[:, None] == block_ids[None, :]
    inner = place - jnp.sum(jnp.where(match, starts[None, :], 0), axis=1)
    live = jnp.ones((rows_total,), bool)
    level = jnp.sum(jnp.where(match, levels[None, :], 0), axis=1)
    return (owner, inner, level, live)


def attend(query, sec_keys, sec_values, hist_keys, hist_values, live, scale):
    count, size = query.shape
    sources, each, _ = sec_keys.shape
    key_parts = divisor_near(sources, max(1, 2048 // each))
    key_blocks = sec_keys.reshape(key_parts, sources // key_parts * each, size)
    value_blocks = sec_values.reshape(key_parts, sources // key_parts * each, size)
    query_parts = divisor_near(count, 512)
    query_blocks = query.reshape(query_parts, count // query_parts, size)

    def one_block(block):
        scores = jnp.dot(block, hist_keys.T, preferred_element_type=jnp.float32) * scale
        scores = jnp.where(live[None, :], scores, -1e30)
        top = jnp.max(scores, axis=1, keepdims=True)
        weights = jnp.where(live[None, :], jnp.exp(scores - top), 0.0)
        total = jnp.sum(weights, axis=1, keepdims=True)
        acc = jnp.dot(weights.astype(jnp.bfloat16), hist_values, preferred_element_type=jnp.float32)

        def step(carry, pair):
            top_now, total_now, acc_now = carry
            key_block, value_block = pair
            fresh = jnp.dot(block, key_block.T, preferred_element_type=jnp.float32) * scale
            newer = jnp.maximum(top_now, jnp.max(fresh, axis=1, keepdims=True))
            fade = jnp.exp(top_now - newer)
            weights_now = jnp.exp(fresh - newer)
            total_next = total_now * fade + jnp.sum(weights_now, axis=1, keepdims=True)
            acc_next = acc_now * fade + jnp.dot(
                weights_now.astype(jnp.bfloat16), value_block, preferred_element_type=jnp.float32
            )
            return ((newer, total_next, acc_next), None)

        (top, total, acc), _ = lax.scan(step, (top, total, acc), (key_blocks, value_blocks))
        return (acc / total).astype(jnp.bfloat16)

    return lax.map(one_block, query_blocks).reshape(count, size)


def shards(
    queries,
    keys,
    values,
    history,
    levels,
    patch_two,
    patch_four,
    patch_sixteen,
    mod_scale,
    mod_shift,
    kv_weight,
    key_gain,
):
    groups = lax.axis_size("seq")
    device = lax.axis_index("seq")
    tok_dev, width = queries.shape
    head_dim = key_gain.shape[0]
    heads = width // head_dim
    q_split = max(groups // heads, 1)
    per_group = max(heads // groups, 1)
    head_groups = heads // per_group
    q_rows = tok_dev // q_split
    positions = history.shape[1]
    scale = head_dim ** (-0.5)
    everything = lax.all_gather(history, "seq", axis=1, tiled=True)
    owner, inner, level, live = history_rows(levels, positions)
    tokens_two = level_tokens(everything, patch_two, 2)
    tokens_four = level_tokens(everything, patch_four, 4)
    tokens_sixteen = level_tokens(everything, patch_sixteen, 16)
    rows_total = owner.shape[0]
    row_parts = divisor_near(rows_total, 512)

    def project(index):
        own, inn, lev = index
        pick_two = jnp.take(
            tokens_two, own * (positions // 2) + jnp.minimum(inn, positions // 2 - 1), axis=0
        )
        pick_four = jnp.take(
            tokens_four, own * (positions // 4) + jnp.minimum(inn, positions // 4 - 1), axis=0
        )
        pick_sixteen = jnp.take(
            tokens_sixteen, own * (positions // 16) + jnp.minimum(inn, positions // 16 - 1), axis=0
        )
        hidden = jnp.where(
            (lev == 2)[:, None], pick_two, jnp.where((lev == 4)[:, None], pick_four, pick_sixteen)
        )
        feats = hidden.astype(jnp.float32)
        mean = jnp.mean(feats, axis=1, keepdims=True)
        centered = feats - mean
        var = jnp.mean(centered * centered, axis=1, keepdims=True)
        normed = (centered * lax.rsqrt(var + EPS) * (1.0 + mod_scale) + mod_shift).astype(
            jnp.bfloat16
        )
        return jnp.dot(normed, kv_weight, preferred_element_type=jnp.float32).astype(jnp.bfloat16)

    share = lax.map(
        project,
        (owner.reshape(row_parts, -1), inner.reshape(row_parts, -1), level.reshape(row_parts, -1)),
    )
    share = share.reshape(rows_total, kv_weight.shape[1])
    pairs = jnp.concatenate(
        [
            keys.reshape(tok_dev, head_groups, per_group, head_dim),
            values.reshape(tok_dev, head_groups, per_group, head_dim),
        ],
        axis=-1,
    )
    full = lax.all_gather(share, "seq", axis=1, tiled=True)
    ordered = full.reshape(rows_total, head_dim, 2, heads).transpose(0, 3, 2, 1)
    mine = lax.dynamic_index_in_dim(
        ordered.reshape(rows_total, head_groups, per_group, 2, head_dim),
        device // q_split,
        axis=1,
        keepdims=False,
    )
    history_kv = key_normed(mine, key_gain)
    rows_each = pairs.shape[0]
    outgoing = jnp.broadcast_to(
        pairs.transpose(1, 0, 2, 3)[:, None],
        (head_groups, q_split, rows_each, per_group, 2 * head_dim),
    )
    outgoing = outgoing.reshape(groups, rows_each, per_group * 2 * head_dim)
    sending = (
        queries.reshape(q_split, q_rows, head_groups, per_group * head_dim)
        .transpose(2, 0, 1, 3)
        .reshape(groups, q_rows, per_group * head_dim)
    )
    got_queries, got_pairs = (
        lax.all_to_all(sending, "seq", split_axis=0, concat_axis=0, tiled=True),
        lax.all_to_all(outgoing, "seq", split_axis=0, concat_axis=0, tiled=True),
    )
    results = []
    for item in range(per_group):
        query = got_queries[:, :, item * head_dim : (item + 1) * head_dim].reshape(
            groups * q_rows, head_dim
        )
        base = item * 2 * head_dim
        sec_keys = got_pairs[:, :, base : base + head_dim]
        sec_values = got_pairs[:, :, base + head_dim : base + 2 * head_dim]
        hist_keys = history_kv[:, item, :head_dim]
        hist_values = history_kv[:, item, head_dim:]
        results.append(attend(query, sec_keys, sec_values, hist_keys, hist_values, live, scale))
    mixed = jnp.concatenate(results, axis=-1).reshape(groups, q_rows, per_group * head_dim)
    returned = lax.all_to_all(mixed, "seq", split_axis=0, concat_axis=0, tiled=True)
    return (
        returned.reshape(head_groups, q_split, q_rows, per_group * head_dim)
        .transpose(1, 2, 0, 3)
        .reshape(tok_dev, width)
    )


def solution(mesh):
    return jax.shard_map(
        shards,
        mesh=mesh,
        in_specs=(
            P(("video", "seq"), None),
            P(("video", "seq"), None),
            P(("video", "seq"), None),
            P(None, ("video", "seq")),
            P("video"),
            P(),
            P(),
            P(),
            P(),
            P(),
            P(None, "seq"),
            P(),
        ),
        out_specs=P(("video", "seq"), None),
        check_vma=False,
    )
```

profile of v0, /device:TPU:1, one launch (start us, length us, event | category | flops | bytes accessed | tf_op | source)
XLA Modules:
  0.0 173.6 jit_solution(1475694497328513225)
XLA Ops:
  6.5 1.3 copy.75
  7.8 0.9 copy.77
  8.7 6.4 %all-to-all-start = ((bf16[8,128,256]{2,1,0:T(8,128)(2,1)}), bf16[8,128,256]{2,1,0:T(8,128)(2,1)}, u32[]{:S(2)}, u32[]{:S(2)}) async-start(bf16[8,128,256]{2,1,0:T(8,128)(2,1)} %bitcast.162), calls=%async_computation | async-start | bytes 1048576 | tf_op jit(solution)/shard_map/all_to_all | solution.py:173
  15.1 21.4 %all-gather = bf16[8,64,16]{1,2,0:T(8,128)(2,1)S(1)} all-gather(bf16[1,64,16]{1,2,0:T(8,128)(2,1)S(1)} %bitcast.177), channel_id=1, replica_groups=mesh['video'=4,'seq'=8] {'seq'}, dimensions={0}, use_global_device_ids=true | all-gather | bytes 18432 | tf_op jit(solution)/shard_map/all_gather | solution.py:109
  37.6 0.6 pad_clamp_fusion.2
  38.3 0.6 pad_clamp_fusion.1
  39.6 0.7 copy.68
  40.3 0.6 compare_and_fusion.2
  40.9 2.2 %reshape.309 = bf16[128,8,2,128]{3,2,1,0:T(2,128)(2,1)} reshape(bf16[128,2048]{1,0:T(8,128)(2,1)} %param.17) | data formatting | bytes 1048576 | tf_op jit(solution)/shard_map/reshape | solution.py:147
  43.1 2.2 %reshape.310 = bf16[128,8,2,128]{3,2,1,0:T(2,128)(2,1)} reshape(bf16[128,2048]{1,0:T(8,128)(2,1)} %param.18) | data formatting | bytes 1048576 | tf_op jit(solution)/shard_map/reshape | solution.py:148
  45.3 1.7 convolution_convert_fusion
  47.1 4.6 %gather_fusion = bf16[136,3072]{1,0:T(8,128)(2,1)} fusion(bf16[256,3072]{1,0:T(8,128)(2,1)} %convolution_convert_fusion, s32[1024]{0:T(1024)} %pad_clamp_fusion.2), kind=kCustom, calls=%fused_computation | custom fusion | bytes 1671712 | tf_op jit(solution)/shard_map/while/body/eval_jaxpr/jit(_take)/gather | solution.py:119
  51.7 1.3 convolution_convert_fusion.1
  53.0 4.3 %gather_fusion.1 = bf16[136,3072]{1,0:T(8,128)(2,1)} fusion(bf16[128,3072]{1,0:T(8,128)(2,1)} %convolution_convert_fusion.1, s32[1024]{0:T(1024)} %pad_clamp_fusion.1), kind=kCustom, calls=%fused_computation.1 | custom fusion | bytes 1671712 | tf_op jit(solution)/shard_map/while/body/eval_jaxpr/jit(_take)/gather | solution.py:122
  57.2 1.8 %convolution_convert_fusion.2 = bf16[32,3072]{1,0:T(8,128)(2,1)S(1)} fusion(bf16[32,256]{0,1:T(8,128)(2,1)S(1)} %bitcast.170, bf16[256,3072]{1,0:T(8,128)(2,1)} %param.23), kind=kOutput, calls=%fused_computation.63 | convolution fusion | flops 50429952 | bytes 1785856 | tf_op jit(solution)/shard_map/dot_general | solution.py:29
  59.1 2.1 %gather_fusion.2 = bf16[136,3072]{1,0:T(8,128)(2,1)} fusion(bf16[32,3072]{1,0:T(8,128)(2,1)S(1)} %convolution_convert_fusion.2, s32[1024]{0:T(1024)} %pad_clamp_fusion), kind=kCustom, calls=%fused_computation.2 | custom fusion | bytes 1671712 | tf_op jit(solution)/shard_map/while/body/eval_jaxpr/jit(_take)/gather | solution.py:125
  61.3 3.3 %convert_reduce_fusion = (f32[136]{0:T(256)S(1)}, bf16[136,3072]{1,0:T(8,128)(2,1)}) fusion(bf16[136,3072]{1,0:T(8,128)(2,1)} %gather_fusion.2, pred[136]{0:T(512)(128)(4,1)S(1)} %copy-done.13, bf16[136,3072]{1,0:T(8,128)(2,1)} %gather_fusion.1, pred[136]{0:T(512)(128)(4,1)S(1)} %copy-done.12, pred[136]{0:T(512)(128)(4,1)S(1)} %copy-done.14, ...), kind=kLoop, calls=%fused_computation.65 | loop fusion | flops 2924408 | bytes 3343560 | tf_op jit(solution)/shard_map/while/body/eval_jaxpr/reduce_sum | solution.py:132
  64.5 2.1 %maximum_bitcast_fusion = bf16[8,128,2,256]{3,2,0,1:T(2,128)(2,1)} fusion(bf16[128,8,2,128]{3,2,1,0:T(2,128)(2,1)S(1)} %copy-done.3, bf16[128,8,2,128]{3,2,1,0:T(2,128)(2,1)S(1)} %copy-done.2), kind=kLoop, calls=%fused_computation.73 | loop fusion | flops 2097152 | bytes 2097152 | tf_op jit(solution)/shard_map/transpose | solution.py:163
  66.6 2.5 %reshape.344 = bf16[8,128,512]{2,0,1:T(8,128)(2,1)} reshape(bf16[8,128,2,256]{3,2,0,1:T(2,128)(2,1)} %maximum_bitcast_fusion) | data formatting | bytes 2097152 | tf_op jit(solution)/shard_map/reshape;broadcast_in_dim | solution.py:166
  69.2 2.6 %copy.74 = bf16[8,128,512]{2,1,0:T(8,128)(2,1)} copy(bf16[8,128,512]{2,0,1:T(8,128)(2,1)} %reshape.344) | data formatting | bytes 2097152 | tf_op jit(solution)/shard_map/reshape;broadcast_in_dim | solution.py:166
  72.2 4.3 %all-to-all-start.1 = ((bf16[8,128,512]{2,1,0:T(8,128)(2,1)}), bf16[8,128,512]{2,1,0:T(8,128)(2,1)}, u32[]{:S(2)}, u32[]{:S(2)}) async-start(bf16[8,128,512]{2,1,0:T(8,128)(2,1)} %copy.74), calls=%async_computation.1 | async-start | bytes 2097152 | tf_op jit(solution)/shard_map/all_to_all | solution.py:174
  76.6 2.5 %convolution_convert_fusion.3 = bf16[136,512]{1,0:T(8,128)(2,1)} fusion(bf16[3072,512]{1,0:T(8,128)(2,1)S(1)} %copy-done, bf16[136,3072]{1,0:T(8,128)(2,1)} %get-tuple-element.191, f32[3072]{0:T(1024)S(1)} %copy-done.18, f32[3072]{0:T(1024)S(1)} %broadcast_add_fusion, f32[136]{0:T(256)S(1)} %add_rsqrt_fusion.1, f32[136]{0:T(256)S(1)} %broadcast_multiply_fusion), kind=kOutput, calls=%fused_computation.72 | convolution fusion | flops 430395392 | bytes 4146240 | tf_op jit(solution)/shard_map/while/body/eval_jaxpr/dot_general | solution.py:138
  79.1 1.9 %fusion.63 = (bf16[8,128,128]{2,1,0:T(8,128)(2,1)}, bf16[8,128,128]{2,1,0:T(8,128)(2,1)}) fusion(bf16[8,128,256]{2,1,0:T(8,128)(2,1)} %all-to-all-done), kind=kLoop, calls=%fused_computation.126 | loop fusion | bytes 1048576 | tf_op jit(solution)/shard_map/slice | solution.py:178
  81.0 30.2 %all-to-all-done.1 = bf16[8,128,512]{2,1,0:T(8,128)(2,1)} async-done(((bf16[8,128,512]{2,1,0:T(8,128)(2,1)}), bf16[8,128,512]{2,1,0:T(8,128)(2,1)}, u32[]{:S(2)}, u32[]{:S(2)}) %all-to-all-start.1) | async-done | bytes 1048608 | tf_op jit(solution)/shard_map/all_to_all | solution.py:174
  111.2 2.1 %fusion.62 = (bf16[8,128,128]{2,1,0:T(8,128)(2,1)}, bf16[8,128,128]{2,1,0:T(8,128)(2,1)}, bf16[8,128,128]{2,1,0:T(8,128)(2,1)S(1)}, bf16[8,128,128]{2,1,0:T(8,128)(2,1)}) fusion(bf16[8,128,512]{2,1,0:T(8,128)(2,1)} %all-to-all-done.1), kind=kLoop, calls=%fused_computation.125 | loop fusion | bytes 2097152 | tf_op jit(solution)/shard_map/slice | solution.py:183
  113.3 3.6 %copy.69 = bf16[136,4096]{0,1:T(8,128)(2,1)} copy(bf16[136,4096]{1,0:T(8,128)(2,1)} %all-gather.3.cloned.1.call-done) | data formatting | bytes 2228224 | tf_op jit(solution)/shard_map/all_gather | solution.py:152
  116.9 4.4 %copy.70 = bf16[136,16,2,128]{3,0,2,1:T(8,128)(2,1)} copy(bf16[136,16,2,128]{0,1,2,3:T(8,128)(2,1)} %bitcast.161) | data formatting | bytes 2228224 | tf_op jit(solution)/shard_map/transpose | solution.py:153
  121.4 0.9 dynamic-slice_bitcast_fusion
  122.6 0.7 broadcast.257.clone.1
  123.3 9.7 %while.18 = (s32[]{:T(128)}, bf16[2,512,128]{2,1,0:T(8,128)(2,1)}, bf16[2,512,128]{2,1,0:T(8,128)(2,1)}, bf16[136,128]{1,0:T(8,128)(2,1)S(1)}, bf16[136,128]{1,0...) while((s32[]{:T(128)}, bf16[2,512,128]{2,1,0:T(8,128)(2,1)}, ...), condition=%wide.region_12.13_spmd, body=%wide.region_7.12_spmd.sunk | while | flops 308961280 | bytes 9727601 | solution.py:81
  123.3 1.1 fusion.99
  124.5 1.5 multiply_reduce_fusion.4
  127.0 1.2 fusion.102
  128.2 1.1 fusion.99
  129.3 1.5 multiply_reduce_fusion.4
  131.8 1.2 fusion.102
  133.0 0.7 broadcast.257.clone
  133.8 9.5 %while.19 = (s32[]{:T(128)}, bf16[2,512,128]{2,1,0:T(8,128)(2,1)}, bf16[2,512,128]{2,1,0:T(8,128)(2,1)}, bf16[136,128]{1,0:T(8,128)(2,1)S(1)}, bf16[136,128]{1,0...) while((s32[]{:T(128)}, bf16[2,512,128]{2,1,0:T(8,128)(2,1)}, ...), condition=%wide.region_18.19_spmd, body=%wide.region_13.18_spmd.sunk | while | flops 308961280 | bytes 9727601 | solution.py:81
  133.8 1.1 fusion.108
  134.9 1.4 multiply_reduce_fusion.5
  137.3 1.2 fusion.111
  138.5 1.1 fusion.108
  139.6 1.4 multiply_reduce_fusion.5
  142.0 1.2 fusion.111
  143.2 1.1 pad_maximum_fusion
  144.3 18.4 %all_to_all.15 = bf16[8,128,256]{2,1,0:T(8,128)(2,1)} all-to-all(bf16[8,128,256]{2,1,0:T(8,128)(2,1)S(1)} %pad_maximum_fusion), channel_id=1, replica_groups=mesh['video'=4,'seq'=8] {'seq'}, dimensions={0} | all-to-all | bytes 1048576 | tf_op jit(solution)/shard_map/all_to_all | solution.py:188
  162.7 2.1 %copy.72 = bf16[8,128,256]{1,2,0:T(8,128)(2,1)} copy(bf16[8,128,256]{2,1,0:T(8,128)(2,1)} %all_to_all.15) | data formatting | bytes 1048576 | tf_op jit(solution)/shard_map/all_to_all | solution.py:188
  164.7 2.0 %copy.73 = bf16[128,2048]{1,0:T(8,128)(2,1)} copy(bf16[128,2048]{0,1:T(8,128)(2,1)} %bitcast.163) | data formatting | bytes 1048576 | tf_op jit(solution)/shard_map/reshape | solution.py:192
  (91 shorter events, 6.4 us)
Async XLA Ops:
  6.5 70.1 %copy-start = (bf16[3072,512]{1,0:T(8,128)(2,1)S(1)}, bf16[3072,512]{1,0:T(8,128)(2,1)}, u32[]{:S(2)}) copy-start(bf16[3072,512]{1,0:T(8,128)(2,1)} %param.26) | copy-start | bytes 9437188
  6.5 8.6 %copy-start.10 = (bf16[16,64]{1,0:T(8,128)(2,1)S(1)}, bf16[16,64]{1,0:T(8,128)(2,1)}, u32[]{:S(2)}) copy-start(bf16[16,64]{1,0:T(8,128)(2,1)} %param.19) | copy-start | bytes 6148
  6.5 30.4 %copy-start.17 = (s32[8]{0:T(128)S(1)}, s32[8]{0:T(128)}, u32[]{:S(2)}) copy-start(s32[8]{0:T(128)} %param.20) | copy-start | bytes 100
  8.7 63.4 %all-to-all-start = ((bf16[8,128,256]{2,1,0:T(8,128)(2,1)}), bf16[8,128,256]{2,1,0:T(8,128)(2,1)}, u32[]{:S(2)}, u32[]{:S(2)}) async-start(bf16[8,128,256]{2,1,0:T(8,128)(2,1)} %bitcast.162), calls=%async_computation | async-start | bytes 1048576 | tf_op jit(solution)/shard_map/all_to_all | solution.py:173
  40.3 5.0 %copy-start.8 = (bf16[32,3072]{1,0:T(8,128)(2,1)S(1)}, bf16[32,3072]{1,0:T(8,128)(2,1)}, u32[]{:S(2)}) copy-start(bf16[32,3072]{1,0:T(8,128)(2,1)} %param.21) | copy-start | bytes 589828
  47.1 4.6 %copy-start.4 = (bf16[64,3072]{1,0:T(8,128)(2,1)S(1)}, bf16[64,3072]{1,0:T(8,128)(2,1)}, u32[]{:S(2)}) copy-start(bf16[64,3072]{1,0:T(8,128)(2,1)} %param.22) | copy-start | bytes 1179652
  53.0 4.3 %copy-start.5 = (bf16[32,16,16]{0,2,1:T(8,128)(2,1)S(1)}, bf16[32,16,16]{0,2,1:T(8,128)(2,1)}, u32[]{:S(2)}) copy-start(bf16[32,16,16]{0,2,1:T(8,128)(2,1)} %copy.68) | copy-start | bytes 49156
  59.0 2.2 %copy-start.11 = (pred[136]{0:T(512)(128)(4,1)S(1)}, pred[136]{0:T(512)(128)(4,1)}, u32[]{:S(2)}) copy-start(pred[136]{0:T(512)(128)(4,1)} %get-tuple-element.210) | copy-start | bytes 412
  59.0 2.2 %copy-start.12 = (pred[136]{0:T(512)(128)(4,1)S(1)}, pred[136]{0:T(512)(128)(4,1)}, u32[]{:S(2)}) copy-start(pred[136]{0:T(512)(128)(4,1)} %get-tuple-element.211) | copy-start | bytes 412
  59.1 2.2 %copy-start.13 = (pred[136]{0:T(512)(128)(4,1)S(1)}, pred[136]{0:T(512)(128)(4,1)}, u32[]{:S(2)}) copy-start(pred[136]{0:T(512)(128)(4,1)} %get-tuple-element.212) | copy-start | bytes 412
  59.1 2.2 %copy-start.14 = (pred[136]{0:T(512)(128)(4,1)S(1)}, pred[136]{0:T(512)(128)(4,1)}, u32[]{:S(2)}) copy-start(pred[136]{0:T(512)(128)(4,1)} %get-tuple-element.221) | copy-start | bytes 412
  59.1 2.2 %copy-start.15 = (pred[136]{0:T(512)(128)(4,1)S(1)}, pred[136]{0:T(512)(128)(4,1)}, u32[]{:S(2)}) copy-start(pred[136]{0:T(512)(128)(4,1)} %get-tuple-element.222) | copy-start | bytes 412
  61.2 3.3 %copy-start.2 = (bf16[128,8,2,128]{3,2,1,0:T(2,128)(2,1)S(1)}, bf16[128,8,2,128]{3,2,1,0:T(2,128)(2,1)}, u32[]{:S(2)}) copy-start(bf16[128,8,2,128]{3,2,1,0:T(2,128)(2,1)} %reshape.309) | copy-start | bytes 1572868
  61.2 3.3 %copy-start.3 = (bf16[128,8,2,128]{3,2,1,0:T(2,128)(2,1)S(1)}, bf16[128,8,2,128]{3,2,1,0:T(2,128)(2,1)}, u32[]{:S(2)}) copy-start(bf16[128,8,2,128]{3,2,1,0:T(2,128)(2,1)} %reshape.310) | copy-start | bytes 1572868
  66.6 5.5 %copy-start.9 = (f32[3072]{0:T(1024)S(1)}, f32[3072]{0:T(1024)}, u32[]{:S(2)}) copy-start(f32[3072]{0:T(1024)} %param.24) | copy-start | bytes 36868
  69.2 2.6 %copy-start.1 = (bf16[136,3072]{1,0:T(8,128)(2,1)S(1)}, bf16[136,3072]{1,0:T(8,128)(2,1)}, u32[]{:S(2)}) copy-start(bf16[136,3072]{1,0:T(8,128)(2,1)} %get-tuple-element.191) | copy-start | bytes 2506756
  69.2 7.4 %copy-start.18 = (f32[3072]{0:T(1024)S(1)}, f32[3072]{0:T(1024)}, u32[]{:S(2)}) copy-start(f32[3072]{0:T(1024)} %param.25) | copy-start | bytes 36868
  72.2 39.0 %all-to-all-start.1 = ((bf16[8,128,512]{2,1,0:T(8,128)(2,1)}), bf16[8,128,512]{2,1,0:T(8,128)(2,1)}, u32[]{:S(2)}, u32[]{:S(2)}) async-start(bf16[8,128,512]{2,1,0:T(8,128)(2,1)} %copy.74), calls=%async_computation.1 | async-start | bytes 2097152 | tf_op jit(solution)/shard_map/all_to_all | solution.py:174
  76.5 36.8 %all-gather.3.cloned.1.call-start = ((), (), s32[]{:S(2)}) async-start(), calls=%async_computation.3 | async-start | bytes 1253376 | tf_op jit(solution)/shard_map/all_gather | solution.py:152
  116.9 5.5 %copy-start.16 = (f32[128]{0:T(128)S(1)}, f32[128]{0:T(128)}, u32[]{:S(2)}) copy-start(f32[128]{0:T(128)} %param.27) | copy-start | bytes 1540
  126.0 1.0 copy-start.7
  130.9 1.0 copy-start.7
  136.3 1.0 copy-start.6
  141.1 1.0 copy-start.6
Sparse Core Ops, SparseCore 0:
  79.2 33.6 all-gather.2
where the time goes:
time: 176 us; the launch traced here: 174 us
  local copies, waits for them, and re-layouts  42.8 us (24%)
  blocking collectives  39.8 us (23%)
  waiting for transfers between devices  30.3 us (17%)
  matrix products  23.8 us (14%)
  between operations  13.6 us (8%)
  other arithmetic  12.5 us (7%)
  starting transfers between devices  10.8 us (6%)
    all_to_all x1, waiting for transfers between devices, shards(): lax.all_to_all(outgoing, 'seq', split_axis=0, concat_axis=0, tiled=True)  30.2 us
    all_gather x1, blocking collectives, shards(): everything = lax.all_gather(history, 'seq', axis=1, tiled=True)  21.4 us
    all_to_all x1, blocking collectives, shards(): lax.all_to_all(mixed, 'seq', split_axis=0, concat_axis=0, tiled=True)  18.4 us
    all_to_all x1, starting transfers between devices, shards(): lax.all_to_all(sending, 'seq', split_axis=0, concat_axis=0, tiled=True)  6.38 us
    dot_general x4, matrix products, step(): jnp.dot(block, key_block.T, preferred_element_type=jnp.float32) * scale  5.93 us
    another operation x2, local copies, waits for them, and re-layouts, shards(): outgoing = outgoing.reshape(groups, rows_each, per_group * 2 * head_dim)  5.12 us
    dot_general x4, matrix products, step(): jnp.dot(weights_now.astype(jnp.bfloat16), value_block, preferred_element_...  4.81 us
    dot_general x3, matrix products, level_tokens(): jnp.dot(grouped, weight, preferred_element_type=jnp.float32)  4.8 us
  transfers between devices with their start and end apart: 3, of which 1 were waited for; matrix products, arithmetic and copies ran while one was open for 24% of the time, Pallas kernels for 0%

commit v1 on v0

--- a/solution.py
+++ b/solution.py
@@ -1,6 +1,10 @@
+import functools
+
 import jax
 import jax.numpy as jnp
 from jax import lax
+from jax.experimental import pallas as pl
+from jax.experimental.pallas import tpu as pltpu
 from jax.sharding import PartitionSpec as P
 
 EPS = 1e-06
@@ -32,7 +36,8 @@
 def history_rows(levels, positions):
     groups = levels.shape[0]
     counts = positions // levels
-    ends = jnp.cumsum(counts)
+    before = jnp.arange(groups)[None, :] <= jnp.arange(groups)[:, None]
+    ends = jnp.sum(jnp.where(before, counts[None, :], 0), axis=1)
     starts = ends - counts
     block_ids = jnp.arange(groups, dtype=jnp.int32)
     rows_total = 17 * positions * groups // 64
@@ -193,9 +198,457 @@
     )
 
 
+def joint_kernel(
+    dims,
+    levels_ref,
+    history_ref,
+    scale_ref,
+    shift_ref,
+    gain_ref,
+    queries_ref,
+    keys_ref,
+    values_ref,
+    two_ref,
+    four_ref,
+    sixteen_ref,
+    weight_ref,
+    out_ref,
+    raw,
+    patches,
+    weight,
+    spread,
+    hidden,
+    share_out,
+    share_in,
+    qbuf,
+    kbuf,
+    vbuf,
+    obuf,
+    load_sem,
+    own_sem,
+    hist_send,
+    hist_recv,
+    share_send,
+    share_recv,
+    kv_send,
+    kv_recv,
+    q_send,
+    q_recv,
+    o_send,
+    o_recv,
+):
+    n, per, hd, rows, padded, positions, channels, off4, off16 = dims
+    tok = queries_ref.shape[0]
+    wide = per * hd
+    half = padded // 2
+    heads = n * per
+    chan = hd // n
+    kinds = 2 * per
+    model = hidden.shape[1]
+    bf, f32 = jnp.bfloat16, jnp.float32
+    me = lax.axis_index("seq")
+
+    def partner(i):
+        return n // 2 + (1 - 2 * (i % 2)) * (i // 2)
+
+    def target(i):
+        return lax.rem(me + partner(i), n)
+
+    def origin(i):
+        return lax.rem(me + n - partner(i), n)
+
+    def lanes(index):
+        return pl.ds(pl.multiple_of(index * wide, 128), wide)
+
+    def band(index):
+        return pl.ds(pl.multiple_of(index * tok, 16), tok)
+
+    def remote(src, dst, send, recv, device):
+        return pltpu.make_async_remote_copy(
+            src_ref=src,
+            dst_ref=dst,
+            send_sem=send,
+            recv_sem=recv,
+            device_id={"seq": device},
+            device_id_type=pl.DeviceIdType.MESH,
+        )
+
+    def hist_copy(device, source):
+        return remote(
+            raw.at[source], raw.at[source], hist_send.at[device], hist_recv.at[source], device
+        )
+
+    def key_copy(device, source):
+        return remote(
+            keys_ref.at[:, lanes(device)],
+            kbuf.at[band(source), :],
+            kv_send.at[0, device],
+            kv_recv.at[0, source],
+            device,
+        )
+
+    def value_copy(device, source):
+        return remote(
+            values_ref.at[:, lanes(device)],
+            vbuf.at[band(source), :],
+            kv_send.at[1, device],
+            kv_recv.at[1, source],
+            device,
+        )
+
+    def query_copy(device, source):
+        return remote(
+            queries_ref.at[:, lanes(device)],
+            qbuf.at[source],
+            q_send.at[device],
+            q_recv.at[source],
+            device,
+        )
+
+    def share_copy(device, source):
+        return remote(
+            share_out.at[device],
+            share_in.at[source],
+            share_send.at[device],
+            share_recv.at[source],
+            device,
+        )
+
+    def out_copy(device, source):
+        return remote(
+            obuf.at[device],
+            out_ref.at[:, lanes(source)],
+            o_send.at[device],
+            o_recv.at[source],
+            device,
+        )
+
+    n2, n4, n16 = two_ref.shape[0], four_ref.shape[0], sixteen_ref.shape[0]
+    loads = [
+        pltpu.make_async_copy(two_ref, patches.at[pl.ds(0, n2), :], load_sem.at[0]),
+        pltpu.make_async_copy(four_ref, patches.at[pl.ds(off4, n4), :], load_sem.at[1]),
+        pltpu.make_async_copy(sixteen_ref, patches.at[pl.ds(off16, n16), :], load_sem.at[2]),
+        pltpu.make_async_copy(weight_ref, weight, load_sem.at[3]),
+    ]
+    own = [
+        pltpu.make_async_copy(keys_ref.at[:, lanes(me)], kbuf.at[band(me), :], own_sem.at[0]),
+        pltpu.make_async_copy(values_ref.at[:, lanes(me)], vbuf.at[band(me), :], own_sem.at[1]),
+        pltpu.make_async_copy(queries_ref.at[:, lanes(me)], qbuf.at[me], own_sem.at[2]),
+    ]
+
+    barrier = pltpu.get_barrier_semaphore()
+
+    @pl.loop(1, n)
+    def _(i):
+        pl.semaphore_signal(
+            barrier, inc=1, device_id={"seq": target(i)}, device_id_type=pl.DeviceIdType.MESH
+        )
+
+    for copy in loads + own:
+        copy.start()
+    gap = off16 - off4 - n4
+    if gap:
+        patches[off4 + n4 : off16, :] = jnp.zeros((gap, model), bf)
+    raw[me] = jnp.concatenate(
+        [history_ref[...], jnp.zeros((channels, 128 - positions), bf)], axis=1
+    )
+    pl.semaphore_wait(barrier, n - 1)
+
+    @pl.loop(1, n)
+    def _(i):
+        hist_copy(target(i), me).start()
+
+    @pl.loop(1, n)
+    def _(i):
+        key_copy(target(i), me).start()
+        value_copy(target(i), me).start()
+
+    spots = n * positions
+    row = lax.broadcasted_iota(jnp.int32, (padded, spots), 0)
+    spot = lax.broadcasted_iota(jnp.int32, (1, spots), 1)
+    start = jnp.int32(0)
+    first = jnp.zeros((1, spots), jnp.int32)
+    factor = jnp.ones((1, spots), jnp.int32)
+    block_levels = []
+    for b in range(n):
+        level = levels_ref[b]
+        block_levels.append(level)
+        inside = spot // positions == b
+        first = jnp.where(inside, start, first)
+        factor = jnp.where(inside, level, factor)
+        start = start + jnp.where(
+            level == 2, positions // 2, jnp.where(level == 4, positions // 4, positions // 16)
+        )
+    begin = (row - first) * factor
+    local = spot % positions
+    member = jnp.where((begin <= local) & (local < begin + factor), 1.0, 0.0).astype(bf)
+
+    width = patches.shape[0]
+    column = lax.broadcasted_iota(jnp.int32, (1, width), 1)
+    kind = jnp.where(
+        column < off4,
+        2,
+        jnp.where(column < off4 + n4, 4, jnp.where(column < off16, 1, 16)),
+    )
+    base = jnp.where(column < off4, 0, jnp.where(column < off16, off4, off16))
+    within = column - base
+    owner_channel = jnp.where(
+        kind == 2, within // 2, jnp.where(kind == 4, within // 4, within // 16)
+    )
+    phase = within - owner_channel * kind
+    channel = lax.broadcasted_iota(jnp.int32, (channels, width), 0)
+    expand = jnp.where((channel == owner_channel) & (kind > 1), 1.0, 0.0).astype(bf)
+    at = lax.broadcasted_iota(jnp.int32, (128, width), 0)
+    remainder = jnp.where(kind == 2, at % 2, jnp.where(kind == 4, at % 4, at % 16))
+    fits = remainder == phase
+
+    @pl.loop(1, n)
+    def _(i):
+        hist_copy(origin(i), origin(i)).wait_recv()
+
+    for b in range(n):
+        spreaded = lax.dot_general(
+            raw[b], expand, (((0,), (0,)), ((), ())), preferred_element_type=f32
+        )
+        keep = fits & (kind == block_levels[b])
+        spread[b * positions : (b + 1) * positions, :] = jnp.where(keep, spreaded, 0.0).astype(bf)[
+            :positions
+        ]
+    grouped = jnp.dot(member, spread[...], preferred_element_type=f32).astype(bf)
+    for copy in loads[:3]:
+        copy.wait()
+    step = 512 if model % 512 == 0 else model
+    total = jnp.zeros((padded, 1), f32)
+    for c in range(0, model, step):
+        tokens = jnp.dot(
+            grouped, patches[:, c : c + step], preferred_element_type=f32
+        ).astype(bf)
+        hidden[:, c : c + step] = tokens
+        total = total + jnp.sum(tokens.astype(f32), axis=1, keepdims=True)
+    mean = total / model
+    square = jnp.zeros((padded, 1), f32)
+    for c in range(0, model, step):
+        centered = hidden[:, c : c + step].astype(f32) - mean
+        square = square + jnp.sum(centered * centered, axis=1, keepdims=True)
+    inverse = lax.rsqrt(square / model + EPS)
+    loads[3].wait()
+    projected = jnp.zeros((padded, weight.shape[1]), f32)
+    for c in range(0, model, step):
+        centered = hidden[:, c : c + step].astype(f32) - mean
+        normed = (
+            centered * inverse * (1.0 + scale_ref[:, c : c + step]) + shift_ref[:, c : c + step]
+        ).astype(bf)
+        projected = projected + jnp.dot(
+            normed, weight[c : c + step, :], preferred_element_type=f32
+        )
+    share = projected.astype(bf)
+
+    cols = chan * 2 * heads
+    take = lax.broadcasted_iota(jnp.int32, (cols, n * 128), 0)
+    give = lax.broadcasted_iota(jnp.int32, (1, n * 128), 1)
+    lane = give % (kinds * chan)
+    dest = give // 128
+    which = lane // chan
+    wanted = (lane % chan) * 2 * heads + (which // per) * heads + dest * per + which % per
+    order = jnp.where(take == wanted, 1.0, 0.0).astype(bf)
+    low = jnp.dot(share[:half], order, preferred_element_type=f32)
+    high = jnp.dot(share[half:], order, preferred_element_type=f32)
+    both = jnp.where(give % 128 < kinds * chan, low, high).astype(bf)
+    for g in range(n):
+        share_out[g] = both[:, g * 128 : (g + 1) * 128]
+
+    @pl.loop(1, n)
+    def _(i):
+        share_copy(target(i), me).start()
+
+    @pl.loop(1, n)
+    def _(i):
+        query_copy(target(i), me).start()
+
+    share_in[me] = share_out[me]
+    taking = lax.broadcasted_iota(jnp.int32, (128, kinds * hd), 0)
+    giving = lax.broadcasted_iota(jnp.int32, (1, kinds * hd), 1)
+    in_head = giving % hd
+    lane_of = (giving // hd) * chan + in_head % chan
+
+    @pl.loop(1, n)
+    def _(i):
+        share_copy(origin(i), origin(i)).wait_recv()
+
+    low = jnp.zeros((half, kinds * hd), f32)
+    high = jnp.zeros((half, kinds * hd), f32)
+    for s in range(n):
+        from_s = in_head // chan == s
+        put_low = jnp.where((taking == lane_of) & from_s, 1.0, 0.0).astype(bf)
+        put_high = jnp.where((taking == lane_of + kinds * chan) & from_s, 1.0, 0.0).astype(bf)
+        low = low + jnp.dot(share_in[s], put_low, preferred_element_type=f32)
+        high = high + jnp.dot(share_in[s], put_high, preferred_element_type=f32)
+    gathered = jnp.concatenate([low, high], axis=0)
+    section = n * tok
+    for h in range(per):
+        key = gathered[:, h * hd : (h + 1) * hd]
+        norm = lax.rsqrt(jnp.mean(key * key, axis=1, keepdims=True) + EPS)
+        kbuf[section:, h * hd : (h + 1) * hd] = (key * norm * gain_ref[...]).astype(bf)
+        vbuf[section:, h * hd : (h + 1) * hd] = gathered[
+            :, (per + h) * hd : (per + h + 1) * hd
+        ].astype(bf)
+
+    for copy in own:
+        copy.wait()
+
+    @pl.loop(1, n)
+    def _(i):
+        key_copy(origin(i), origin(i)).wait_recv()
+        value_copy(origin(i), origin(i)).wait_recv()
+
+    rate = hd**-0.5 * 1.4426950408889634
+    live = lax.broadcasted_iota(jnp.int32, (1, padded), 1) < rows
+    across = (((1,), (1,)), ((), ()))
+
+    def attend_block(source):
+        for h in range(per):
+            cut = slice(h * hd, (h + 1) * hd)
+            query = qbuf[source, :, cut]
+            near = lax.dot_general(query, kbuf[:section, cut], across, preferred_element_type=f32)
+            past = lax.dot_general(query, kbuf[section:, cut], across, preferred_element_type=f32)
+            past = jnp.where(live, past, -1e30)
+            top = jnp.maximum(
+                jnp.max(near, axis=1, keepdims=True), jnp.max(past, axis=1, keepdims=True)
+            )
+            near = jnp.exp2((near - top) * rate)
+            past = jnp.exp2((past - top) * rate)
+            total = jnp.sum(near, axis=1, keepdims=True) + jnp.sum(past, axis=1, keepdims=True)
+            mixed = jnp.dot(near.astype(bf), vbuf[:section, cut], preferred_element_type=f32)
+            mixed = mixed + jnp.dot(past.astype(bf), vbuf[section:, cut], preferred_element_type=f32)
+            obuf[source, :, cut] = (mixed / total).astype(bf)
+
+    attend_block(me)
+    own_out = pltpu.make_async_copy(obuf.at[me], out_ref.at[:, lanes(me)], own_sem.at[3])
+    own_out.start()
+
+    @pl.loop(1, n)
+    def _(i):
+        source = origin(i)
+        query_copy(source, source).wait_recv()
+        attend_block(source)
+        out_copy(source, me).start()
+
+    @pl.loop(1, n)
+    def _(i):
+        device = target(i)
+        hist_copy(device, me).wait_send()
+        key_copy(device, me).wait_send()
+        value_copy(device, me).wait_send()
+        share_copy(device, me).wait_send()
+        query_copy(device, me).wait_send()
+        out_copy(device, me).wait_send()
+
+    @pl.loop(1, n)
+    def _(i):
+        out_copy(origin(i), origin(i)).wait_recv()
+
+    own_out.wait()
+
+
+def fits_kernel(groups, tok_dev, width, head_dim, positions):
+    heads = width // head_dim
+    if groups < 2 or groups % 2 or heads % groups or head_dim % groups or tok_dev % 16:
+        return False
+    per_group = heads // groups
+    held = 4 * 2 * groups * tok_dev * per_group * head_dim
+    lanes = 4 * per_group * (head_dim // groups)
+    return held <= 16 * 2**20 and lanes == 128 and head_dim % 128 == 0 and positions <= 128
+
+
+def fused(
+    queries,
+    keys,
+    values,
+    history,
+    levels,
+    patch_two,
+    patch_four,
+    patch_sixteen,
+    mod_scale,
+    mod_shift,
+    kv_weight,
+    key_gain,
+):
+    n = lax.axis_size("seq")
+    tok, width = queries.shape
+    hd = key_gain.shape[0]
+    per = width // hd // n
+    channels, positions = history.shape
+    model = mod_scale.shape[0]
+    rows = 17 * positions * n // 64
+    padded = -(-rows // 32) * 32
+    off4 = patch_two.shape[0]
+    off16 = -(-(off4 + patch_four.shape[0]) // 128) * 128
+    depth = off16 + patch_sixteen.shape[0]
+    dims = (n, per, hd, rows, padded, positions, channels, off4, off16)
+    bf = jnp.bfloat16
+    dma = pltpu.SemaphoreType.DMA
+    vmem = pl.BlockSpec(memory_space=pltpu.VMEM)
+    anywhere = pl.BlockSpec(memory_space=pl.ANY)
+    return pl.pallas_call(
+        functools.partial(joint_kernel, dims),
+        out_shape=jax.ShapeDtypeStruct((tok, width), bf),
+        in_specs=[pl.BlockSpec(memory_space=pltpu.SMEM)] + [vmem] * 4 + [anywhere] * 7,
+        out_specs=anywhere,
+        scratch_shapes=[
+            pltpu.VMEM((n, channels, 128), bf),
+            pltpu.VMEM((depth, model), bf),
+            pltpu.VMEM(kv_weight.shape, bf),
+            pltpu.VMEM((n * positions, depth), bf),
+            pltpu.VMEM((padded, model), bf),
+            pltpu.VMEM((n, padded // 2, 128), bf),
+            pltpu.VMEM((n, padded // 2, 128), bf),
+            pltpu.VMEM((n, tok, per * hd), bf),
+            pltpu.VMEM((n * tok + padded, per * hd), bf),
+            pltpu.VMEM((n * tok + padded, per * hd), bf),
+            pltpu.VMEM((n, tok, per * hd), bf),
+            dma((4,)),
+            dma((4,)),
+            dma((n,)),
+            dma((n,)),
+            dma((n,)),
+            dma((n,)),
+            dma((2, n)),
+            dma((2, n)),
+            dma((n,)),
+            dma((n,)),
+            dma((n,)),
+            dma((n,)),
+        ],
+        compiler_params=pltpu.CompilerParams(
+            collective_id=0, has_side_effects=True, vmem_limit_bytes=48 * 2**20
+        ),
+    )(
+        levels,
+        history,
+        mod_scale.reshape(1, -1),
+        mod_shift.reshape(1, -1),
+        key_gain.reshape(1, -1),
+        queries,
+        keys,
+        values,
+        patch_two,
+        patch_four,
+        patch_sixteen,
+        kv_weight,
+    )
+
+
+def route(*args):
+    queries, history, key_gain = args[0], args[3], args[11]
+    groups = lax.axis_size("seq")
+    chosen = fits_kernel(groups, *queries.shape, key_gain.shape[0], history.shape[1])
+    return (fused if chosen else shards)(*args)
+
+
 def solution(mesh):
     return jax.shard_map(
-        shards,
+        route,
         mesh=mesh,
         in_specs=(
             P(("video", "seq"), None),

time: 176 us -> 66.4 us (0.38); the launches traced: 174 us -> 66 us
  Pallas kernels: 0 us -> 55.3 us
  blocking collectives: 39.8 us -> 0 us
  local copies, waits for them, and re-layouts: 42.8 us -> 10.7 us
  waiting for transfers between devices: 30.3 us -> 0 us
  matrix products: 23.8 us -> 0 us
  between operations: 13.6 us -> 0.02 us
  other arithmetic: 12.5 us -> 0 us
  starting transfers between devices: 10.8 us -> 0 us
    pallas_call x0 -> x1, Pallas kernels: none -> 55.3 us  [fused(): pl.pallas_call(functools.partial(joint_kernel, dims), out_shape=jax.Shape...]
    all_to_all x2 -> x0, waiting for transfers between devices: 30.2 us -> none  [the longest x1 30.2 us: shards(): lax.all_to_all(outgoing, 'seq', split_axis=0, concat_axis=0, tiled=True)]
    dot_general x20 -> x0, matrix products: 23.8 us -> none  [the longest x4 5.93 us: step(): jnp.dot(block, key_block.T, preferred_element_type=jnp.float32) * scale]
    all_gather x1 -> x0, blocking collectives: 21.4 us -> none  [shards(): everything = lax.all_gather(history, 'seq', axis=1, tiled=True)]
    all_to_all x1 -> x0, blocking collectives: 18.4 us -> none  [shards(): lax.all_to_all(mixed, 'seq', split_axis=0, concat_axis=0, tiled=True)]
    gather x3 -> x0, local copies, waits for them, and re-layouts: 11 us -> none  [the longest x1 4.63 us: project(): jnp.take(tokens_two, own * (positions // 2) + jnp.minimum(inn, positions...]
    all_to_all x2 -> x0, starting transfers between devices: 10.7 us -> none  [the longest x1 6.38 us: shards(): lax.all_to_all(sending, 'seq', split_axis=0, concat_axis=0, tiled=True)]
    unnamed x37 -> x23, local copies, waits for them, and re-layouts: 1.6 us -> 10.7 us
  transfers between devices with their start and end apart: 3 -> 0, of which waited for: 1 -> 0; matrix products, arithmetic and copies ran while one was open for 24% -> 0% of each run, Pallas kernels for 0% -> 0%
where the time goes in v1:
time: 66.4 us; the launch traced here: 66 us
  Pallas kernels  55.3 us (83%)
  local copies, waits for them, and re-layouts  10.7 us (16%)
    pallas_call x1, Pallas kernels, fused(): pl.pallas_call(functools.partial(joint_kernel, dims), out_shape=jax.Shape...  55.3 us
    unnamed x23, local copies, waits for them, and re-layouts  10.7 us

profile of v1, /device:TPU:1, one launch (start us, length us, event | category | flops | bytes accessed | tf_op | source)
XLA Modules:
  0.0 66.0 jit_solution(7559834567942902355)
XLA Ops:
  0.0 0.0 copy-start
  0.0 1.4 %copy-done = bf16[256,3072]{1,0:T(8,128)(2,1)S(1)} copy-done((bf16[256,3072]{1,0:T(8,128)(2,1)S(1)}, bf16[256,3072]{1,0:T(8,128)(2,1)}, u32[]{:S(2)}) %copy-start) | copy-done | bytes 1572888
  1.4 0.0 copy-start.1
  1.4 1.0 %copy-done.1 = bf16[128,2048]{1,0:T(8,128)(2,1)S(1)} copy-done((bf16[128,2048]{1,0:T(8,128)(2,1)S(1)}, bf16[128,2048]{1,0:T(8,128)(2,1)}, u32[]{:S(2)}) %copy-start.1) | copy-done | bytes 524312
  2.5 0.0 copy-start.2
  2.5 1.0 %copy-done.2 = bf16[128,2048]{1,0:T(8,128)(2,1)S(1)} copy-done((bf16[128,2048]{1,0:T(8,128)(2,1)S(1)}, bf16[128,2048]{1,0:T(8,128)(2,1)}, u32[]{:S(2)}) %copy-start.2) | copy-done | bytes 524312
  3.5 0.0 copy-start.3
  3.5 1.0 %copy-done.3 = bf16[128,2048]{1,0:T(8,128)(2,1)S(1)} copy-done((bf16[128,2048]{1,0:T(8,128)(2,1)S(1)}, bf16[128,2048]{1,0:T(8,128)(2,1)}, u32[]{:S(2)}) %copy-start.3) | copy-done | bytes 524312
  4.5 0.0 copy-start.4
  4.5 1.0 %copy-done.4 = bf16[64,3072]{1,0:T(8,128)(2,1)S(1)} copy-done((bf16[64,3072]{1,0:T(8,128)(2,1)S(1)}, bf16[64,3072]{1,0:T(8,128)(2,1)}, u32[]{:S(2)}) %copy-start.4) | copy-done | bytes 393240
  5.5 0.0 copy-start.5
  5.5 0.9 %copy-done.5 = bf16[32,3072]{1,0:T(8,128)(2,1)S(1)} copy-done((bf16[32,3072]{1,0:T(8,128)(2,1)S(1)}, bf16[32,3072]{1,0:T(8,128)(2,1)}, u32[]{:S(2)}) %copy-start.5) | copy-done | bytes 196632
  6.5 0.0 copy-start.6
  6.5 0.7 %copy-done.6 = f32[3072]{0:T(1024)S(1)} copy-done((f32[3072]{0:T(1024)S(1)}, f32[3072]{0:T(1024)}, u32[]{:S(2)}) %copy-start.6) | copy-done | bytes 12312
  7.2 0.0 copy-start.7
  7.2 0.7 %copy-done.7 = f32[3072]{0:T(1024)S(1)} copy-done((f32[3072]{0:T(1024)S(1)}, f32[3072]{0:T(1024)}, u32[]{:S(2)}) %copy-start.7) | copy-done | bytes 12312
  7.9 0.0 copy-start.8
  7.9 0.7 %copy-done.8 = bf16[16,64]{1,0:T(8,128)(2,1)S(1)} copy-done((bf16[16,64]{1,0:T(8,128)(2,1)S(1)}, bf16[16,64]{1,0:T(8,128)(2,1)}, u32[]{:S(2)}) %copy-start.8) | copy-done | bytes 2072
  8.6 0.0 copy-start.9
  8.6 0.7 copy-done.9
  9.2 0.0 copy-start.10
  9.2 0.7 copy-done.10
  9.9 55.3 %shard_map.118 = bf16[128,2048]{1,0:T(8,128)(2,1)S(1)} custom-call(s32[8]{0:T(128)S(1)} %copy-done.9, bf16[16,64]{1,0:T(8,128)(2,1)S(1)} %copy-done.8, f32[1,3072]{1,0:T(1,128)S(1)} %bitcast.3, f32[1,3072]{1,0:T(1,128)S(1)} %bitcast.4, f32[1,128]{1,0:T(1,128)S(1)} %bitcast.5, bf16[128,2048]{1,0:T(8,128)(2,1)S(1)} %copy-done.1, ...), custom_call_target="tpu_custom_call" | custom-call | tf_op jit(solution)/shard_map/pallas_call | solution.py:593
  65.2 0.8 %copy.14 = bf16[128,2048]{1,0:T(8,128)(2,1)} copy(bf16[128,2048]{1,0:T(8,128)(2,1)S(1)} %shard_map.118) | data formatting | bytes 1048576
Async XLA Ops:
  0.0 1.4 %copy-start = (bf16[256,3072]{1,0:T(8,128)(2,1)S(1)}, bf16[256,3072]{1,0:T(8,128)(2,1)}, u32[]{:S(2)}) copy-start(bf16[256,3072]{1,0:T(8,128)(2,1)} %sixteen_ref.1) | copy-start | bytes 4718596
  1.4 1.0 %copy-start.1 = (bf16[128,2048]{1,0:T(8,128)(2,1)S(1)}, bf16[128,2048]{1,0:T(8,128)(2,1)}, u32[]{:S(2)}) copy-start(bf16[128,2048]{1,0:T(8,128)(2,1)} %queries_ref.1) | copy-start | bytes 1572868
  2.5 1.0 %copy-start.2 = (bf16[128,2048]{1,0:T(8,128)(2,1)S(1)}, bf16[128,2048]{1,0:T(8,128)(2,1)}, u32[]{:S(2)}) copy-start(bf16[128,2048]{1,0:T(8,128)(2,1)} %keys_ref.1) | copy-start | bytes 1572868
  3.5 1.0 %copy-start.3 = (bf16[128,2048]{1,0:T(8,128)(2,1)S(1)}, bf16[128,2048]{1,0:T(8,128)(2,1)}, u32[]{:S(2)}) copy-start(bf16[128,2048]{1,0:T(8,128)(2,1)} %values_ref.1) | copy-start | bytes 1572868
  4.5 1.0 %copy-start.4 = (bf16[64,3072]{1,0:T(8,128)(2,1)S(1)}, bf16[64,3072]{1,0:T(8,128)(2,1)}, u32[]{:S(2)}) copy-start(bf16[64,3072]{1,0:T(8,128)(2,1)} %four_ref.1) | copy-start | bytes 1179652
  5.5 0.9 %copy-start.5 = (bf16[32,3072]{1,0:T(8,128)(2,1)S(1)}, bf16[32,3072]{1,0:T(8,128)(2,1)}, u32[]{:S(2)}) copy-start(bf16[32,3072]{1,0:T(8,128)(2,1)} %two_ref.1) | copy-start | bytes 589828
  6.5 0.7 %copy-start.6 = (f32[3072]{0:T(1024)S(1)}, f32[3072]{0:T(1024)}, u32[]{:S(2)}) copy-start(f32[3072]{0:T(1024)} %param.20) | copy-start | bytes 36868
  7.2 0.7 %copy-start.7 = (f32[3072]{0:T(1024)S(1)}, f32[3072]{0:T(1024)}, u32[]{:S(2)}) copy-start(f32[3072]{0:T(1024)} %param.21) | copy-start | bytes 36868
  7.9 0.7 %copy-start.8 = (bf16[16,64]{1,0:T(8,128)(2,1)S(1)}, bf16[16,64]{1,0:T(8,128)(2,1)}, u32[]{:S(2)}) copy-start(bf16[16,64]{1,0:T(8,128)(2,1)} %history_ref.1) | copy-start | bytes 6148
  8.6 0.7 copy-start.9
  9.2 0.7 copy-start.10

commit v2 on v1

--- a/solution.py
+++ b/solution.py
@@ -589,7 +589,7 @@
     bf = jnp.bfloat16
     dma = pltpu.SemaphoreType.DMA
     vmem = pl.BlockSpec(memory_space=pltpu.VMEM)
-    anywhere = pl.BlockSpec(memory_space=pl.ANY)
+    anywhere = pl.BlockSpec(memory_space=pltpu.HBM)
     return pl.pallas_call(
         functools.partial(joint_kernel, dims),
         out_shape=jax.ShapeDtypeStruct((tok, width), bf),
@@ -621,7 +621,7 @@
             dma((n,)),
         ],
         compiler_params=pltpu.CompilerParams(
-            collective_id=0, has_side_effects=True, vmem_limit_bytes=48 * 2**20
+            collective_id=0, has_side_effects=True, vmem_limit_bytes=63 * 2**20
         ),
     )(
         levels,

time: 66.4 us -> 57.7 us (0.87)
  local copies, waits for them, and re-layouts: 10.7 us -> 1.88 us
    unnamed x23 -> x1, local copies, waits for them, and re-layouts: 10.7 us -> 1.88 us
where the time goes in v2:
time: 57.7 us; the launch traced here: 57.5 us
  Pallas kernels  55.6 us (96%)
  local copies, waits for them, and re-layouts  1.88 us (3%)
    pallas_call x1, Pallas kernels, fused(): pl.pallas_call(functools.partial(joint_kernel, dims), out_shape=jax.Shape...  55.6 us
    unnamed x1, local copies, waits for them, and re-layouts  1.88 us

profile of v2, /device:TPU:1, one launch (start us, length us, event | category | flops | bytes accessed | tf_op | source)
XLA Modules:
  0.0 57.5 jit_solution(13588870489046459627)
XLA Ops:
  0.0 55.6 %shard_map.118 = bf16[128,2048]{1,0:T(8,128)(2,1)} custom-call(s32[8]{0:T(128)} %levels_ref.1, bf16[16,64]{1,0:T(8,128)(2,1)} %history_ref.1, f32[1,3072]{1,0:T(1,128)} %bitcast.3, f32[1,3072]{1,0:T(1,128)} %bitcast.4, f32[1,128]{1,0:T(1,128)} %bitcast.5, bf16[128,2048]{1,0:T(8,128)(2,1)} %queries_ref.1, bf16[128,2048]{1,0:T(8,128)(2,1)} %keys_ref.1, ...), custom_call_target="tpu_custom_call" | custom-call | tf_op jit(solution)/shard_map/pallas_call | solution.py:593
  55.6 1.9 %copy.14 = bf16[128,2048]{1,0:T(8,128)(2,1)} copy(bf16[128,2048]{1,0:T(8,128)(2,1)} %shard_map.118) | data formatting | bytes 1048576
